TPU v7x, 512 devices: a whole 4x4x16 slice. The times are simulated.
512 devices in a mesh: vox: 64 (over z, x_hi, core), tm: 4 (over y), mod: 2 (over x_lo).
Axes of the slice: x: 4 (x_hi: 2, x_lo: 2; x = x_hi * 2 + x_lo), y: 4, z: 16, core: 2. Of those that a mesh axis runs over, the one named last changes fastest.
Arguments:
- scans: bfloat16 [2, 16384, 48, 512], P('mod', 'vox', None, 'tm'), may hold values from -6 to 6
- spatial_init: float32 [2, 16384, 128], P('mod', 'vox'), may hold values from -6 to 6
- time_init: float32 [512, 128], P('tm'), may hold values from -0.09375 to 0.09375
- subject_init: float32 [48, 128], replicated, may hold values from -6 to 6
- hrf_kernel: float32 [16], replicated, may hold values from 0.05 to 0.5
- kept_blocks: int32 [48, 32], P(None, 'tm'), may hold values 0 or 1
Outputs:
- spatial_factors: float32 [2, 16384, 128], P('mod', 'vox')
- time_factors: float32 [512, 128], P('tm')
- subject_factors: float32 [48, 128], replicated
All inputs are finite; a program needn't handle non-finite values. No bound on the sum of `kept_blocks` on one device may be relied on, other than what follows from the above.
Results may differ from a plain program's by a relative error of at most 0.003.
Values sent between devices are 32-bit elements; how exact they have to be, the bound alone decides.
A program may use at most 64 MiB of HBM per device.

v0:
```python
import jax
import jax.numpy as jnp
from jax import lax
from jax.sharding import PartitionSpec as P

RIDGE = 0.1
EPS = 1e-06


def shifted(block, axis, distance):
    devices = range(lax.axis_size(axis))
    route = [(i - distance, i) for i in devices if i - distance in devices]
    return lax.ppermute(block, axis, route)


def ridge_solve(right_side, gram):
    eye_mat = jnp.eye(gram.shape[0], dtype=gram.dtype)
    factor = jnp.linalg.cholesky(gram + RIDGE * eye_mat)
    return jax.scipy.linalg.cho_solve((factor, True), right_side.T).T


def hgram(left, right):
    return jnp.dot(left.T, right, precision=lax.Precision.HIGHEST)


def conv_causal(series, kernel):
    reach = kernel.shape[0]
    count = series.shape[0]
    tail_part = series[count - (reach - 1) :]
    before = shifted(tail_part, "tm", 1)
    padded = jnp.concatenate([before, series])
    summed = jnp.zeros_like(series)
    for lag in range(reach):
        summed = summed + kernel[lag] * padded[reach - 1 - lag : reach - 1 - lag + count]
    return summed


def conv_adjoint(series, kernel):
    reach = kernel.shape[0]
    count = series.shape[0]
    head_part = series[: reach - 1]
    after = shifted(head_part, "tm", -1)
    padded = jnp.concatenate([series, after])
    summed = jnp.zeros_like(series)
    for lag in range(reach):
        summed = summed + kernel[lag] * padded[lag : lag + count]
    return summed


def per_device(scans, spatial_init, time_init, subject_init, hrf_kernel, kept_blocks):
    is_fmri = lax.axis_index("mod") == 0
    row_count, subj_count, tr_count = (scans.shape[1], scans.shape[2], scans.shape[3])
    rank_count = subject_init.shape[1]
    total_rows = row_count * lax.axis_size("vox")
    total_trs = tr_count * lax.axis_size("tm")
    factor_t = jnp.where(is_fmri, conv_causal(time_init, hrf_kernel), time_init)
    block_len = tr_count // kept_blocks.shape[1]
    kept_tr = jnp.logical_or(
        jnp.repeat(kept_blocks, block_len, axis=1) > 0, jnp.logical_not(is_fmri)
    )
    khatri = (
        (subject_init[:, None, :] * factor_t[None, :, :])
        .astype(jnp.bfloat16)
        .reshape(subj_count * tr_count, rank_count)
    )
    signal = scans[0].reshape(row_count, subj_count * tr_count)
    previous = spatial_init[0].astype(jnp.bfloat16)
    modeled = lax.dot_general(
        previous, khatri, (((1,), (1,)), ((), ())), preferred_element_type=jnp.float32
    )
    filled = jnp.where(
        kept_tr.reshape(1, subj_count * tr_count), signal.astype(jnp.float32), modeled
    ).astype(jnp.bfloat16)
    mttkrp_part = jnp.dot(filled, khatri, preferred_element_type=jnp.float32)
    tgram_part = hgram(factor_t, factor_t)
    mttkrp, time_gram = lax.psum((mttkrp_part, tgram_part), "tm")
    subj_gram = hgram(subject_init, subject_init)
    updated = ridge_solve(mttkrp, subj_gram * time_gram)
    rgram_part = hgram(updated, updated)
    khatri2 = (
        (updated[:, None, :] * subject_init[None, :, :])
        .astype(jnp.bfloat16)
        .reshape(row_count * subj_count, rank_count)
    )
    proj = lax.dot_general(
        filled.reshape(row_count * subj_count, tr_count),
        khatri2,
        (((0,), (0,)), ((), ())),
        preferred_element_type=jnp.float32,
    )
    adjoint = jnp.where(is_fmri, conv_adjoint(proj, hrf_kernel), proj)
    tgram_terms = rgram_part * subj_gram
    time_rhs, gram_t = lax.psum((adjoint, tgram_terms), ("vox", "mod"))
    raw = total_rows * ridge_solve(time_rhs, gram_t)
    sumsq = lax.psum(jnp.sum(raw * raw, axis=0), "tm")
    time_factors = raw / jnp.sqrt(sumsq / total_trs + EPS)
    scale_c = (2.0 * total_rows * total_trs) ** (-0.5)
    scaled_eeg = time_factors * scale_c
    scaled_t = jnp.where(is_fmri, conv_causal(scaled_eeg, hrf_kernel), scaled_eeg)
    khatri3 = (updated[:, None, :] * scaled_t[None, :, :]).astype(jnp.bfloat16)
    subj_part = lax.dot_general(
        filled.reshape(row_count, subj_count, tr_count),
        khatri3,
        (((0, 2), (0, 1)), ((), ())),
        preferred_element_type=jnp.float32,
    )
    sgram_part = hgram(scaled_t, scaled_t)
    row_gram = lax.psum(rgram_part, "vox")
    scaled_gram = lax.psum(sgram_part, "tm")
    leading = jnp.logical_and(lax.axis_index("vox") == 0, lax.axis_index("tm") == 0)
    gram_term = jnp.where(leading, row_gram * scaled_gram, 0.0)
    subject_rhs, gram_c = lax.psum((subj_part, gram_term), ("vox", "tm", "mod"))
    subject_factors = ridge_solve(subject_rhs, gram_c)
    return (updated[None], time_factors, subject_factors)


def solution(mesh):
    return jax.shard_map(
        per_device,
        mesh=mesh,
        in_specs=(
            P("mod", "vox", None, "tm"),
            P("mod", "vox", None),
            P("tm", None),
            P(),
            P(),
            P(None, "tm"),
        ),
        out_specs=(P("mod", "vox", None), P("tm", None), P()),
        check_vma=False,
    )
```

profile of v0, /device:TPU:1, one launch (start us, length us, event | category | flops | bytes accessed | tf_op | source)
XLA Modules:
  0.0 1485.5 jit_solution(1407539403140570844)
XLA Ops:
  7.9 4.0 collective-permute-start
  12.6 1.9 fusion.160
  14.6 5.1 copy.23
  20.1 10.2 fusion.98
  31.6 4.8 fusion.4
  36.4 1.7 fusion.163
  38.4 3.1 copy.26
  41.5 5.7 reshape.87
  47.2 50.4 %all-reduce.16.cloned.1.call-done = (f32[256,128]{1,0:T(8,128)}, f32[128,128]{1,0:T(8,128)}) async-done(((f32[256,128]{1,0:T(8,128)}, f32[128,128]{1,0:T(8,128)}), (f32[256,128]{1,0:T(8,128)}, f32[128,128]{1,0:T(8,128)})) %all-reduce.16.cloned.1.call-update) | async-done | bytes 196624 | tf_op jit(solution)/shard_map/psum | solution.py:76
  99.0 11.7 cholesky.59
  112.0 9.8 custom-call.23
  121.9 1.2 fusion.156
  124.0 1.3 copy-done
  126.4 1.3 collective-permute-start.1
  128.6 2.2 collective-permute-done.1
  130.8 10.8 fusion.54
  141.9 322.2 %all-reduce.14.cloned.1.call-done = (f32[128,128]{1,0:T(8,128)}, f32[128,128]{1,0:T(8,128)}) async-done(((f32[128,128]{1,0:T(8,128)}, f32[128,128]{1,0:T(8,128)}), (f32[128,128]{1,0:T(8,128)}, f32[128,128]{1,0:T(8,128)})) %all-reduce.14.cloned.1.call-update) | async-done | bytes 131088 | tf_op jit(solution)/shard_map/psum | solution.py:93
  466.6 12.5 cholesky.70
  479.8 1.3 fusion.139
  481.1 10.6 custom-call.24
  493.2 8.5 psum.67
  502.3 1.3 collective-permute-start.2
  504.4 10.4 fusion.10
  515.7 3.5 copy.32
  519.9 429.4 %all-reduce.8.cloned.1.call-done = f32[128,128]{1,0:T(8,128)} async-done(((f32[128,128]{1,0:T(8,128)}), f32[128,128]{1,0:T(8,128)}) %all-reduce.8.cloned.1.call-update) | async-done | bytes 65552 | tf_op jit(solution)/shard_map/psum | solution.py:108
  949.3 54.3 %all-reduce.10.cloned.1.call-done = f32[128,128]{1,0:T(8,128)} async-done(((f32[128,128]{1,0:T(8,128)}), f32[128,128]{1,0:T(8,128)}) %all-reduce.10.cloned.1.call-update) | async-done | bytes 65552 | tf_op jit(solution)/shard_map/psum | solution.py:109
  1003.6 1.5 multiply_select_fusion
  1005.2 3.2 fusion.5
  1008.4 106.8 %psum.71 = f32[48,128]{1,0:T(8,128)S(1)} all-reduce(f32[48,128]{1,0:T(8,128)S(1)} %fusion.5), channel_id=1, replica_groups=mesh['vox'=64,'tm'=4,'mod'=2] {'vox','tm','mod'}, use_global_device_ids=true, to_apply=%region_11.13 | all-reduce | flops 6144 | bytes 49152 | tf_op jit(solution)/shard_map/psum | solution.py:112
  1115.1 337.9 %all-reduce.12.cloned.1.call-done = f32[128,128]{1,0:T(8,128)} async-done(((f32[128,128]{1,0:T(8,128)}), f32[128,128]{1,0:T(8,128)}) %all-reduce.12.cloned.1.call-update) | async-done | bytes 65552 | tf_op jit(solution)/shard_map/psum | solution.py:112
  1455.0 11.7 cholesky.81
  1468.0 9.8 custom-call.25
  (61 shorter events, 20.7 us)
Async XLA Ops:
  7.2 90.5 %all-reduce.16.cloned.1.call-start = ((), (), s32[]{:S(2)}) async-start(), calls=%async_computation.4 | async-start | bytes 393216 | tf_op jit(solution)/shard_map/psum | solution.py:76
  7.9 12.2 collective-permute-start
  14.6 5.5 copy-start.3
  14.6 16.6 %copy-start.1 = (f32[48,128]{1,0:T(8,128)S(1)}, f32[48,128]{1,0:T(8,128)}, u32[]{:S(2)}) copy-start(f32[48,128]{1,0:T(8,128)} %param.10) | copy-start | bytes 73732
  14.6 17.0 %copy-start.2 = (f32[1,256,128]{2,1,0:T(8,128)S(1)}, f32[1,256,128]{2,1,0:T(8,128)}, u32[]{:S(2)}) copy-start(f32[1,256,128]{2,1,0:T(8,128)} %param.8) | copy-start | bytes 393220
  38.1 425.9 %all-reduce.14.cloned.1.call-start = ((), (), s32[]{:S(2)}) async-start(), calls=%async_computation.3 | async-start | bytes 262144 | tf_op jit(solution)/shard_map/psum | solution.py:93
  123.4 1.9 copy-start
  126.4 4.4 collective-permute-start.1
  141.6 807.7 %all-reduce.8.cloned.1.call-start = ((), (), s32[]{:S(2)}) async-start(), calls=%async_computation | async-start | bytes 131072 | tf_op jit(solution)/shard_map/psum | solution.py:108
  502.3 2.1 collective-permute-start.2
  504.3 499.4 %all-reduce.10.cloned.1.call-start = ((), (), s32[]{:S(2)}) async-start(), calls=%async_computation.1 | async-start | bytes 131072 | tf_op jit(solution)/shard_map/psum | solution.py:109
  515.7 937.4 %all-reduce.12.cloned.1.call-start = ((), (), s32[]{:S(2)}) async-start(), calls=%async_computation.2 | async-start | bytes 131072 | tf_op jit(solution)/shard_map/psum | solution.py:112
Sparse Core Ops, SparseCore 0:
  38.3 59.3 all-reduce.15
  141.7 322.2 all-reduce.13
  504.4 444.8 all-reduce.7
  951.5 52.1 all-reduce.9
  1009.8 443.1 all-reduce.11
where the time goes:
time: 1490 us
  waiting for transfers between devices  1200 us (81%)
  blocking collectives  115 us (8%)
  other arithmetic  109 us (7%)
  local copies, waits for them, and re-layouts  23.8 us (2%)
  matrix products  18.6 us (1%)
    psum x1, waiting for transfers between devices, per_device(): row_gram = lax.psum(rgram_part, 'vox')  429 us
    psum x1, waiting for transfers between devices, per_device(): subject_rhs, gram_c = lax.psum((subj_part, gram_term), ('vox', 'tm', 'mod'))  338 us
    psum x1, waiting for transfers between devices, per_device(): time_rhs, gram_t = lax.psum((adjoint, tgram_terms), ('vox', 'mod'))  322 us
    psum x1, blocking collectives, per_device(): subject_rhs, gram_c = lax.psum((subj_part, gram_term), ('vox', 'tm', 'mod'))  107 us
    psum x1, waiting for transfers between devices, per_device(): scaled_gram = lax.psum(sgram_part, 'tm')  54.3 us
    psum x1, waiting for transfers between devices, per_device(): mttkrp, time_gram = lax.psum((mttkrp_part, tgram_part), 'tm')  50.4 us
    another operation x9, other arithmetic, ridge_solve(): factor = jnp.linalg.cholesky(gram + RIDGE * eye_mat)  38 us
    another operation x6, other arithmetic, ridge_solve(): return jax.scipy.linalg.cho_solve((factor, True), right_side.T).T  32.9 us
  transfers between devices with their start and end apart: 8, of which 7 were waited for; matrix products, arithmetic and copies ran while one was open for 2% of the time, Pallas kernels for 0%

commit v1 on v0

--- a/solution.py
+++ b/solution.py
@@ -105,7 +105,7 @@
         preferred_element_type=jnp.float32,
     )
     sgram_part = hgram(scaled_t, scaled_t)
-    row_gram = lax.psum(rgram_part, "vox")
+    row_gram = jnp.sum(lax.all_gather(rgram_part, "vox"), axis=0)
     scaled_gram = lax.psum(sgram_part, "tm")
     leading = jnp.logical_and(lax.axis_index("vox") == 0, lax.axis_index("tm") == 0)
     gram_term = jnp.where(leading, row_gram * scaled_gram, 0.0)

time: 1490 us -> 1150 us (0.77)
  waiting for transfers between devices: 1200 us -> 854 us
    psum x1 -> x0, waiting for transfers between devices: 429 us -> none  [per_device(): row_gram = lax.psum(rgram_part, 'vox')]
    all_gather x0 -> x1, waiting for transfers between devices: none -> 91.9 us  [per_device(): row_gram = jnp.sum(lax.all_gather(rgram_part, 'vox'), axis=0)]
  transfers between devices with their start and end apart: 8 -> 8, of which waited for: 7 -> 7; matrix products, arithmetic and copies ran while one was open for 2% -> 6% of each run, Pallas kernels for 0% -> 0%
where the time goes in v1:
time: 1150 us; the launch traced here: 1140 us
  waiting for transfers between devices  854 us (74%)
  blocking collectives  116 us (10%)
  other arithmetic  112 us (10%)
  local copies, waits for them, and re-layouts  23.7 us (2%)
  matrix products  16.7 us (1%)
  between operations  14.8 us (1%)
    psum x1, waiting for transfers between devices, per_device(): subject_rhs, gram_c = lax.psum((subj_part, gram_term), ('vox', 'tm', 'mod'))  339 us
    psum x1, waiting for transfers between devices, per_device(): time_rhs, gram_t = lax.psum((adjoint, tgram_terms), ('vox', 'mod'))  321 us
    psum x1, blocking collectives, per_device(): subject_rhs, gram_c = lax.psum((subj_part, gram_term), ('vox', 'tm', 'mod'))  107 us
    all_gather x1, waiting for transfers between devices, per_device(): row_gram = jnp.sum(lax.all_gather(rgram_part, 'vox'), axis=0)  91.9 us
    psum x1, waiting for transfers between devices, per_device(): mttkrp, time_gram = lax.psum((mttkrp_part, tgram_part), 'tm')  50.4 us
    psum x1, waiting for transfers between devices, per_device(): scaled_gram = lax.psum(sgram_part, 'tm')  48.2 us
    another operation x9, other arithmetic, ridge_solve(): factor = jnp.linalg.cholesky(gram + RIDGE * eye_mat)  38 us
    another operation x6, other arithmetic, ridge_solve(): return jax.scipy.linalg.cho_solve((factor, True), right_side.T).T  32.9 us
  transfers between devices with their start and end apart: 8, of which 7 were waited for; matrix products, arithmetic and copies ran while one was open for 6% of the time, Pallas kernels for 0%

profile of v1, /device:TPU:1, one launch (start us, length us, event | category | flops | bytes accessed | tf_op | source)
XLA Modules:
  0.0 1143.6 jit_solution(12530694061414593140)
XLA Ops:
  7.9 4.0 collective-permute-start
  12.6 1.9 fusion.160
  14.6 5.1 copy.23
  20.1 10.2 fusion.98
  31.6 4.8 fusion.4
  36.4 1.7 fusion.163
  38.4 3.1 copy.26
  41.5 5.7 reshape.87
  47.2 50.4 %all-reduce.13.cloned.1.call-done = (f32[256,128]{1,0:T(8,128)}, f32[128,128]{1,0:T(8,128)}) async-done(((f32[256,128]{1,0:T(8,128)}, f32[128,128]{1,0:T(8,128)}), (f32[256,128]{1,0:T(8,128)}, f32[128,128]{1,0:T(8,128)})) %all-reduce.13.cloned.1.call-update) | async-done | bytes 196624 | tf_op jit(solution)/shard_map/psum | solution.py:76
  99.0 11.7 %cholesky.59 = f32[128,128]{1,0:T(8,128)S(1)} custom-call(f32[128,128]{1,0:T(8,128)S(1)} %copy.21), custom_call_target="Cholesky" | custom-call | tf_op jit(solution)/shard_map/jit(cholesky)/cholesky | solution.py:18
  112.0 9.8 custom-call.23
  124.0 1.3 copy-done
  126.4 1.3 collective-permute-start.1
  128.6 2.2 collective-permute-done.1
  130.8 10.8 fusion.54
  142.6 321.4 %all-reduce.11.cloned.1.call-done = (f32[128,128]{1,0:T(8,128)}, f32[128,128]{1,0:T(8,128)}) async-done(((f32[128,128]{1,0:T(8,128)}, f32[128,128]{1,0:T(8,128)}), (f32[128,128]{1,0:T(8,128)}, f32[128,128]{1,0:T(8,128)})) %all-reduce.11.cloned.1.call-update) | async-done | bytes 131088 | tf_op jit(solution)/shard_map/psum | solution.py:93
  466.6 12.5 %cholesky.70 = f32[128,128]{1,0:T(8,128)S(1)} custom-call(f32[128,128]{1,0:T(8,128)} %copy.25), custom_call_target="Cholesky" | custom-call | tf_op jit(solution)/shard_map/jit(cholesky)/cholesky | solution.py:18
  479.8 1.3 fusion.139
  481.1 10.7 custom-call.24
  493.2 8.9 psum.60
  502.7 1.4 collective-permute-start.2
  504.9 10.4 fusion.10
  516.3 3.4 copy.32
  520.5 91.9 %all-gather.3.cloned.1.call-done = f32[8192,128]{1,0:T(8,128)} async-done(((f32[128,128]{1,0:T(8,128)}), f32[8192,128]{1,0:T(8,128)}) %all-gather.3.cloned.1.call-update) | async-done | bytes 4194320 | tf_op jit(solution)/shard_map/all_gather | solution.py:108
  612.4 2.4 reduce_sum.19
  614.8 48.2 %all-reduce.7.cloned.1.call-done = f32[128,128]{1,0:T(8,128)} async-done(((f32[128,128]{1,0:T(8,128)}), f32[128,128]{1,0:T(8,128)}) %all-reduce.7.cloned.1.call-update) | async-done | bytes 65552 | tf_op jit(solution)/shard_map/psum | solution.py:109
  663.0 1.5 multiply_select_fusion
  664.5 1.3 fusion.5
  665.8 106.7 %psum.63 = f32[48,128]{1,0:T(8,128)S(1)} all-reduce(f32[48,128]{1,0:T(8,128)S(1)} %fusion.5), channel_id=1, replica_groups=mesh['vox'=64,'tm'=4,'mod'=2] {'vox','tm','mod'}, use_global_device_ids=true, to_apply=%region_11.13 | all-reduce | flops 6144 | bytes 49152 | tf_op jit(solution)/shard_map/psum | solution.py:112
  772.5 338.6 %all-reduce.9.cloned.1.call-done = f32[128,128]{1,0:T(8,128)} async-done(((f32[128,128]{1,0:T(8,128)}), f32[128,128]{1,0:T(8,128)}) %all-reduce.9.cloned.1.call-update) | async-done | bytes 65552 | tf_op jit(solution)/shard_map/psum | solution.py:112
  1113.1 11.7 %cholesky.81 = f32[128,128]{1,0:T(8,128)S(1)} custom-call(f32[128,128]{1,0:T(8,128)S(1)} %copy.29), custom_call_target="Cholesky" | custom-call | tf_op jit(solution)/shard_map/jit(cholesky)/cholesky | solution.py:18
  1126.1 9.8 custom-call.25
  (64 shorter events, 22.6 us)
Async XLA Ops:
  7.2 90.5 %all-reduce.13.cloned.1.call-start = ((), (), s32[]{:S(2)}) async-start(), calls=%async_computation.4 | async-start | bytes 393216 | tf_op jit(solution)/shard_map/psum | solution.py:76
  7.9 12.2 %collective-permute-start = (f32[15,128]{1,0:T(8,128)S(1)}, f32[15,128]{1,0:T(8,128)S(1)}, u32[]{:S(2)}, u32[]{:S(2)}) collective-permute-start(f32[15,128]{1,0:T(8,128)S(1)} %slice.266), channel_id=1, source_target_pairs={{0,2},{2,4},{4,6},{1,3},{3,5},{5,7},{8,10},{10,12},{12,14},{9,11},... | collective-permute-start | bytes 23048 | tf_op jit(solution)/shard_map/ppermute | solution.py:13
  14.6 5.5 copy-start.4
  14.6 16.6 %copy-start.2 = (f32[48,128]{1,0:T(8,128)S(1)}, f32[48,128]{1,0:T(8,128)}, u32[]{:S(2)}) copy-start(f32[48,128]{1,0:T(8,128)} %param.10) | copy-start | bytes 73732
  14.6 17.0 %copy-start.3 = (f32[1,256,128]{2,1,0:T(8,128)S(1)}, f32[1,256,128]{2,1,0:T(8,128)}, u32[]{:S(2)}) copy-start(f32[1,256,128]{2,1,0:T(8,128)} %param.8) | copy-start | bytes 393220
  38.1 425.9 %all-reduce.11.cloned.1.call-start = ((), (), s32[]{:S(2)}) async-start(), calls=%async_computation.3 | async-start | bytes 262144 | tf_op jit(solution)/shard_map/psum | solution.py:93
  123.4 1.9 copy-start
  126.4 4.4 collective-permute-start.1
  141.6 470.8 %all-gather.3.cloned.1.call-start = ((), (), s32[]{:S(2)}) async-start(), calls=%async_computation.2 | async-start | bytes 4259840 | tf_op jit(solution)/shard_map/all_gather | solution.py:108
  142.3 520.6 %all-reduce.7.cloned.1.call-start = ((), (), s32[]{:S(2)}) async-start(), calls=%async_computation | async-start | bytes 131072 | tf_op jit(solution)/shard_map/psum | solution.py:109
  502.7 2.2 collective-permute-start.2
  516.2 594.9 %all-reduce.9.cloned.1.call-start = ((), (), s32[]{:S(2)}) async-start(), calls=%async_computation.1 | async-start | bytes 131072 | tf_op jit(solution)/shard_map/psum | solution.py:112
  519.7 144.8 %copy-start.1 = (bf16[256,48,128]{2,1,0:T(8,128)(2,1)S(1)}, bf16[256,48,128]{2,1,0:T(8,128)(2,1)}, u32[]{:S(2)}) copy-start(bf16[256,48,128]{2,1,0:T(8,128)(2,1)} %copy.32) | copy-start | bytes 9437188
Sparse Core Ops, SparseCore 0:
  38.3 59.3 all-reduce.12
  141.7 322.2 all-reduce.10
  467.8 144.4 all-gather.2
  614.6 48.3 all-reduce.6
  668.3 442.8 all-reduce.8

commit v2 on v0

--- a/solution.py
+++ b/solution.py
@@ -90,7 +90,7 @@
     )
     adjoint = jnp.where(is_fmri, conv_adjoint(proj, hrf_kernel), proj)
     tgram_terms = rgram_part * subj_gram
-    time_rhs, gram_t = lax.psum((adjoint, tgram_terms), ("vox", "mod"))
+    time_rhs, gram_t = lax.psum(lax.psum((adjoint, tgram_terms), "vox"), "mod")
     raw = total_rows * ridge_solve(time_rhs, gram_t)
     sumsq = lax.psum(jnp.sum(raw * raw, axis=0), "tm")
     time_factors = raw / jnp.sqrt(sumsq / total_trs + EPS)

time: 1490 us -> 1260 us (0.85)
  waiting for transfers between devices: 1200 us -> 967 us
    psum x2, waiting for transfers between devices: 752 us -> 521 us  [per_device(): time_rhs, gram_t = lax.psum(lax.psum((adjoint, tgram_terms), 'vox'), 'mod')]
where the time goes in v2:
time: 1260 us
  waiting for transfers between devices  967 us (77%)
  blocking collectives  115 us (9%)
  other arithmetic  109 us (9%)
  local copies, waits for them, and re-layouts  23.8 us (2%)
  matrix products  18.6 us (1%)
  between operations  14.8 us (1%)
    psum x2, waiting for transfers between devices, per_device(): time_rhs, gram_t = lax.psum(lax.psum((adjoint, tgram_terms), 'vox'), 'mod')  521 us
    psum x1, waiting for transfers between devices, per_device(): subject_rhs, gram_c = lax.psum((subj_part, gram_term), ('vox', 'tm', 'mod'))  338 us
    psum x1, blocking collectives, per_device(): subject_rhs, gram_c = lax.psum((subj_part, gram_term), ('vox', 'tm', 'mod'))  107 us
    psum x1, waiting for transfers between devices, per_device(): scaled_gram = lax.psum(sgram_part, 'tm')  55 us
    psum x1, waiting for transfers between devices, per_device(): mttkrp, time_gram = lax.psum((mttkrp_part, tgram_part), 'tm')  50.4 us
    another operation x9, other arithmetic, ridge_solve(): factor = jnp.linalg.cholesky(gram + RIDGE * eye_mat)  38 us
    another operation x6, other arithmetic, ridge_solve(): return jax.scipy.linalg.cho_solve((factor, True), right_side.T).T  32.9 us
  transfers between devices with their start and end apart: 8, of which 7 were waited for; matrix products, arithmetic and copies ran while one was open for 2% of the time, Pallas kernels for 0%

profile of v2, /device:TPU:1, one launch (start us, length us, event | category | flops | bytes accessed | tf_op | source)
XLA Modules:
  0.0 1255.8 jit_solution(7703660838256751535)
XLA Ops:
  7.9 4.0 collective-permute-start
  12.6 1.9 fusion.160
  14.6 5.1 copy.23
  20.1 10.2 fusion.98
  31.6 4.8 fusion.4
  36.4 1.7 fusion.163
  38.4 3.1 copy.26
  41.5 5.7 reshape.87
  47.2 50.4 %all-reduce.15.cloned.1.call-done = (f32[256,128]{1,0:T(8,128)}, f32[128,128]{1,0:T(8,128)}) async-done(((f32[256,128]{1,0:T(8,128)}, f32[128,128]{1,0:T(8,128)}), (f32[256,128]{1,0:T(8,128)}, f32[128,128]{1,0:T(8,128)})) %all-reduce.15.cloned.1.call-update) | async-done | bytes 196624 | tf_op jit(solution)/shard_map/psum | solution.py:76
  99.0 11.7 cholesky.59
  112.0 9.8 custom-call.23
  121.9 1.2 fusion.156
  124.0 1.3 copy-done
  126.4 1.3 collective-permute-start.1
  128.6 2.2 collective-permute-done.1
  130.8 10.8 fusion.54
  141.6 476.9 %all-reduce.13.cloned.1.call-done = (f32[128,128]{1,0:T(8,128)}, f32[128,128]{1,0:T(8,128)}, f32[128,128]{1,0:T(8,128)}) async-done(((f32[128,128]{1,0:T(8,128)}, f32[128,128]{1,0:T(8,128)}, f32[128,128]{1,0:T(8,128)}), (f32[128,128]{1,0:T(8,128)}, f32[128,128]{1,0:T(8,128)}, f32[128,128]{1,0:T(8,128)})) %all-reduce.13.cloned.1.call-update) | async-done | bytes 196624 | tf_op jit(solution)/shard_map/psum | solution.py:93
  618.8 44.1 %all-reduce.17.cloned.1.call-done = (f32[128,128]{1,0:T(8,128)}, f32[128,128]{1,0:T(8,128)}) async-done(((f32[128,128]{1,0:T(8,128)}, f32[128,128]{1,0:T(8,128)}), (f32[128,128]{1,0:T(8,128)}, f32[128,128]{1,0:T(8,128)})) %all-reduce.17.cloned.1.call-update) | async-done | bytes 131088 | tf_op jit(solution)/shard_map/psum | solution.py:93
  665.5 12.5 cholesky.70
  678.8 1.3 fusion.139
  680.0 10.6 custom-call.24
  692.1 8.5 psum.83
  701.2 1.3 collective-permute-start.2
  703.3 10.4 fusion.10
  714.7 3.5 copy.32
  718.9 55.0 %all-reduce.9.cloned.1.call-done = f32[128,128]{1,0:T(8,128)} async-done(((f32[128,128]{1,0:T(8,128)}), f32[128,128]{1,0:T(8,128)}) %all-reduce.9.cloned.1.call-update) | async-done | bytes 65552 | tf_op jit(solution)/shard_map/psum | solution.py:109
  773.9 1.5 multiply_select_fusion
  775.4 3.2 fusion.5
  778.6 106.8 %psum.87 = f32[48,128]{1,0:T(8,128)S(1)} all-reduce(f32[48,128]{1,0:T(8,128)S(1)} %fusion.5), channel_id=1, replica_groups=mesh['vox'=64,'tm'=4,'mod'=2] {'vox','tm','mod'}, use_global_device_ids=true, to_apply=%region_13.15 | all-reduce | flops 6144 | bytes 49152 | tf_op jit(solution)/shard_map/psum | solution.py:112
  885.4 338.0 %all-reduce.11.cloned.1.call-done = f32[128,128]{1,0:T(8,128)} async-done(((f32[128,128]{1,0:T(8,128)}), f32[128,128]{1,0:T(8,128)}) %all-reduce.11.cloned.1.call-update) | async-done | bytes 65552 | tf_op jit(solution)/shard_map/psum | solution.py:112
  1225.3 11.7 cholesky.81
  1238.3 9.8 custom-call.25
  (63 shorter events, 20.7 us)
Async XLA Ops:
  7.2 90.5 %all-reduce.15.cloned.1.call-start = ((), (), s32[]{:S(2)}) async-start(), calls=%async_computation.3 | async-start | bytes 393216 | tf_op jit(solution)/shard_map/psum | solution.py:76
  7.9 12.2 collective-permute-start
  14.6 5.5 copy-start.3
  14.6 16.6 %copy-start.1 = (f32[48,128]{1,0:T(8,128)S(1)}, f32[48,128]{1,0:T(8,128)}, u32[]{:S(2)}) copy-start(f32[48,128]{1,0:T(8,128)} %param.10) | copy-start | bytes 73732
  14.6 17.0 %copy-start.2 = (f32[1,256,128]{2,1,0:T(8,128)S(1)}, f32[1,256,128]{2,1,0:T(8,128)}, u32[]{:S(2)}) copy-start(f32[1,256,128]{2,1,0:T(8,128)} %param.8) | copy-start | bytes 393220
  38.1 580.4 %all-reduce.13.cloned.1.call-start = ((), (), s32[]{:S(2)}) async-start(), calls=%async_computation.2 | async-start | bytes 393216 | tf_op jit(solution)/shard_map/psum | solution.py:93
  123.4 1.9 copy-start
  126.4 4.4 collective-permute-start.1
  141.6 521.4 %all-reduce.17.cloned.1.call-start = ((), (), s32[]{:S(2)}) async-start(), calls=%async_computation.4 | async-start | bytes 262144 | tf_op jit(solution)/shard_map/psum | solution.py:93
  618.6 155.3 %all-reduce.9.cloned.1.call-start = ((), (), s32[]{:S(2)}) async-start(), calls=%async_computation | async-start | bytes 131072 | tf_op jit(solution)/shard_map/psum | solution.py:109
  701.2 2.1 collective-permute-start.2
  714.6 508.7 %all-reduce.11.cloned.1.call-start = ((), (), s32[]{:S(2)}) async-start(), calls=%async_computation.1 | async-start | bytes 131072 | tf_op jit(solution)/shard_map/psum | solution.py:112
  714.7 59.2 %copy-start.4 = (f32[128,128]{1,0:T(8,128)S(1)}, f32[128,128]{1,0:T(8,128)}, u32[]{:S(2)}) copy-start(f32[128,128]{1,0:T(8,128)} %get-tuple-element.12) | copy-start | bytes 196612
Sparse Core Ops, SparseCore 0:
  38.3 59.3 all-reduce.14
  141.7 476.7 all-reduce.12
  621.4 41.4 all-reduce.16
  714.7 59.0 all-reduce.8
  780.1 443.2 all-reduce.10
